TPU v7x, 512 devices: a whole 4x8x8 slice. The times are simulated.
512 devices in a mesh: cmp: 32 (over z, x), tgt: 16 (over y, core).
Axes of the slice: x: 4, y: 8, z: 8, core: 2. Of those that a mesh axis runs over, the one named last changes fastest.
Arguments:
- responses: bfloat16 [8192, 1024, 128], P('cmp', 'tgt'), may hold values from -33 to 33
- target_init: bfloat16 [1024, 64], P('tgt'), may hold values from -5 to 5
- condition_factor: bfloat16 [128, 64], replicated, may hold values from -0.5 to 0.5
Outputs:
- compound_factor: float32 [8192, 64], P('cmp')
- target_factor: float32 [1024, 64], P('tgt')
All inputs are finite; a program needn't handle non-finite values.
Results may differ from a plain program's by a relative error of at most 0.0003.
Values sent between devices are 32-bit elements; how exact they have to be, the bound alone decides.
A program may use at most 64 MiB of HBM per device.

v0:
```python
import jax
import jax.numpy as jnp
from jax import lax
from jax.sharding import PartitionSpec as P

ITERS = 5


def gram_of(factor):
    return jnp.dot(
        factor.T, factor, precision=lax.Precision.HIGHEST, preferred_element_type=jnp.float32
    )


def solve_normal(rhs, normal):
    lower = jnp.linalg.cholesky(normal)
    middle = lax.linalg.triangular_solve(lower, rhs, left_side=False, lower=True, transpose_a=True)
    return lax.linalg.triangular_solve(
        lower, middle, left_side=False, lower=True, transpose_a=False
    )


def target_total(partial_gram):
    return lax.psum(partial_gram, "tgt")


def body(responses, target_init, condition_factor):
    cmp_rows = responses.shape[0]
    tgt_rows = responses.shape[1]
    cond_count = responses.shape[2]
    rank_width = condition_factor.shape[1]
    cond = condition_factor.astype(jnp.float32)
    cond_gram = gram_of(cond)
    flat = jnp.dot(
        responses.reshape(cmp_rows * tgt_rows, cond_count),
        condition_factor,
        preferred_element_type=jnp.float32,
    )
    shared = flat.reshape(cmp_rows, tgt_rows, rank_width)

    def fetch():
        return shared

    target_raw = target_init.astype(jnp.float32)
    pending = gram_of(target_raw)
    target_gram = target_total(pending)
    compound_raw = jnp.zeros((cmp_rows, rank_width), jnp.float32)
    compound_gram = jnp.zeros((rank_width, rank_width), jnp.float32)
    for sweep in range(ITERS):
        inner = fetch()
        first = jnp.einsum("ijr,jr->ir", inner, target_raw, precision=lax.Precision.HIGHEST)
        summed = lax.psum(first, "tgt")
        compound_raw = solve_normal(summed, target_gram * cond_gram)
        inner_again = fetch()
        second = jnp.einsum(
            "ijr,ir->jr", inner_again, compound_raw, precision=lax.Precision.HIGHEST
        )
        target_sum, compound_gram = lax.psum((second, gram_of(compound_raw)), "cmp")
        target_raw = solve_normal(target_sum, compound_gram * cond_gram)
        pending = gram_of(target_raw)
        target_gram = target_total(pending)
    compound_count = cmp_rows * lax.axis_size("cmp")
    target_count = tgt_rows * lax.axis_size("tgt")
    compound_factor = (
        compound_raw / jnp.sqrt(jnp.diagonal(compound_gram) / compound_count + 1e-06)[None, :]
    )
    target_factor = target_raw / jnp.sqrt(jnp.diagonal(target_gram) / target_count + 1e-06)[None, :]
    return (compound_factor, target_factor)


def solution(mesh):
    return jax.shard_map(
        body,
        mesh=mesh,
        in_specs=(P("cmp", "tgt", None), P("tgt", None), P()),
        out_specs=(P("cmp", None), P("tgt", None)),
        check_vma=False,
    )
```

profile of v0, /device:TPU:1, one launch (start us, length us, event | category | flops | bytes accessed | tf_op | source)
XLA Modules:
  0.0 1432.1 jit_solution(13418670611447832796)
XLA Ops:
  8.1 6.6 fusion
  21.3 49.6 %psum.147 = f32[64,64]{0,1:T(8,128)S(1)} all-reduce(f32[64,64]{0,1:T(8,128)S(1)} %fusion.112), channel_id=1, replica_groups=mesh['cmp'=32,'tgt'=16] {'tgt'}, use_global_device_ids=true, to_apply=%region_0.0 | all-reduce | flops 4096 | bytes 32768 | tf_op jit(solution)/shard_map/psum | solution.py:24
  83.3 48.6 %all-reduce.11.cloned.1.call-done = f32[256,64]{0,1:T(8,128)} async-done(((f32[256,64]{0,1:T(8,128)}), f32[256,64]{0,1:T(8,128)}) %all-reduce.11.cloned.1.call-update) | async-done | bytes 65552 | tf_op jit(solution)/shard_map/psum | solution.py:52
  133.3 7.7 fusion.18
  141.0 116.3 %all-reduce.4 = (f32[64,64]{0,1:T(8,128)S(1)}, f32[64,64]{0,1:T(8,128)S(1)}) all-reduce(f32[64,64]{0,1:T(8,128)S(1)} %bitcast.303, f32[64,64]{0,1:T(8,128)S(1)} %fusion.30), channel_id=1, replica_groups=mesh['cmp'=32,'tgt'=16] {'cmp'}, use_global_device_ids=true, to_apply=%region_5.9 | all-reduce | flops 8192 | bytes 65536 | tf_op jit(solution)/shard_map/psum | solution.py:58
  257.5 5.8 cholesky.175
  270.2 6.4 fusion.16
  277.3 70.1 %psum.151 = f32[64,64]{0,1:T(8,128)S(1)} all-reduce(f32[64,64]{0,1:T(8,128)S(1)} %fusion.84), channel_id=1, replica_groups=mesh['cmp'=32,'tgt'=16] {'tgt'}, use_global_device_ids=true, to_apply=%region_6.12 | all-reduce | flops 4096 | bytes 32768 | tf_op jit(solution)/shard_map/psum | solution.py:24
  347.5 5.8 cholesky.186
  359.6 42.7 %all-reduce.13.cloned.1.call-done = f32[256,64]{0,1:T(8,128)} async-done(((f32[256,64]{0,1:T(8,128)}), f32[256,64]{0,1:T(8,128)}) %all-reduce.13.cloned.1.call-update) | async-done | bytes 65552 | tf_op jit(solution)/shard_map/psum | solution.py:52
  403.7 7.7 fusion.14
  411.4 116.4 %all-reduce.3 = (f32[64,64]{0,1:T(8,128)S(1)}, f32[64,64]{0,1:T(8,128)S(1)}) all-reduce(f32[64,64]{0,1:T(8,128)S(1)} %bitcast.304, f32[64,64]{0,1:T(8,128)S(1)} %fusion.28), channel_id=1, replica_groups=mesh['cmp'=32,'tgt'=16] {'cmp'}, use_global_device_ids=true, to_apply=%region_9.15 | all-reduce | flops 8192 | bytes 65536 | tf_op jit(solution)/shard_map/psum | solution.py:58
  527.9 5.8 cholesky.197
  540.6 6.4 fusion.12
  547.8 70.2 %psum.155 = f32[64,64]{0,1:T(8,128)S(1)} all-reduce(f32[64,64]{0,1:T(8,128)S(1)} %fusion.74), channel_id=1, replica_groups=mesh['cmp'=32,'tgt'=16] {'tgt'}, use_global_device_ids=true, to_apply=%region_10.16 | all-reduce | flops 4096 | bytes 32768 | tf_op jit(solution)/shard_map/psum | solution.py:24
  618.1 5.8 cholesky.208
  630.1 42.7 %all-reduce.15.cloned.1.call-done = f32[256,64]{0,1:T(8,128)} async-done(((f32[256,64]{0,1:T(8,128)}), f32[256,64]{0,1:T(8,128)}) %all-reduce.15.cloned.1.call-update) | async-done | bytes 65552 | tf_op jit(solution)/shard_map/psum | solution.py:52
  674.4 7.7 fusion.10
  682.1 116.7 %all-reduce.2 = (f32[64,64]{0,1:T(8,128)S(1)}, f32[64,64]{0,1:T(8,128)S(1)}) all-reduce(f32[64,64]{0,1:T(8,128)S(1)} %bitcast.305, f32[64,64]{0,1:T(8,128)S(1)} %fusion.26), channel_id=1, replica_groups=mesh['cmp'=32,'tgt'=16] {'cmp'}, use_global_device_ids=true, to_apply=%region_13.19 | all-reduce | flops 8192 | bytes 65536 | tf_op jit(solution)/shard_map/psum | solution.py:58
  811.6 6.4 fusion.8
  818.7 70.0 %psum.159 = f32[64,64]{0,1:T(8,128)S(1)} all-reduce(f32[64,64]{0,1:T(8,128)S(1)} %fusion.64), channel_id=1, replica_groups=mesh['cmp'=32,'tgt'=16] {'tgt'}, use_global_device_ids=true, to_apply=%region_14.20 | all-reduce | flops 4096 | bytes 32768 | tf_op jit(solution)/shard_map/psum | solution.py:24
  888.9 5.8 cholesky.230
  901.0 42.7 %all-reduce.17.cloned.1.call-done = f32[256,64]{0,1:T(8,128)} async-done(((f32[256,64]{0,1:T(8,128)}), f32[256,64]{0,1:T(8,128)}) %all-reduce.17.cloned.1.call-update) | async-done | bytes 65552 | tf_op jit(solution)/shard_map/psum | solution.py:52
  945.2 7.7 fusion.6
  952.9 116.4 %all-reduce.1 = (f32[64,64]{0,1:T(8,128)S(1)}, f32[64,64]{0,1:T(8,128)S(1)}) all-reduce(f32[64,64]{0,1:T(8,128)S(1)} %bitcast.306, f32[64,64]{0,1:T(8,128)S(1)} %fusion.24), channel_id=1, replica_groups=mesh['cmp'=32,'tgt'=16] {'cmp'}, use_global_device_ids=true, to_apply=%region_17.23 | all-reduce | flops 8192 | bytes 65536 | tf_op jit(solution)/shard_map/psum | solution.py:58
  1069.4 5.8 cholesky.241
  1082.1 6.4 fusion.4
  1089.2 70.1 %psum.163 = f32[64,64]{0,1:T(8,128)S(1)} all-reduce(f32[64,64]{0,1:T(8,128)S(1)} %fusion.54), channel_id=1, replica_groups=mesh['cmp'=32,'tgt'=16] {'tgt'}, use_global_device_ids=true, to_apply=%region_18.24 | all-reduce | flops 4096 | bytes 32768 | tf_op jit(solution)/shard_map/psum | solution.py:24
  1171.5 42.8 %all-reduce.19.cloned.1.call-done = f32[256,64]{0,1:T(8,128)} async-done(((f32[256,64]{0,1:T(8,128)}), f32[256,64]{0,1:T(8,128)}) %all-reduce.19.cloned.1.call-update) | async-done | bytes 65552 | tf_op jit(solution)/shard_map/psum | solution.py:52
  1215.7 7.7 fusion.2
  1223.4 116.2 %all-reduce = (f32[64,64]{0,1:T(8,128)S(1)}, f32[64,64]{0,1:T(8,128)S(1)}) all-reduce(f32[64,64]{0,1:T(8,128)S(1)} %fusion.22, f32[64,64]{0,1:T(8,128)S(1)} %bitcast.307), channel_id=1, replica_groups=mesh['cmp'=32,'tgt'=16] {'cmp'}, use_global_device_ids=true, to_apply=%region_20.26 | all-reduce | flops 8192 | bytes 65536 | tf_op jit(solution)/shard_map/psum | solution.py:58
  1353.9 69.8 %psum.167 = f32[64,64]{1,0:T(8,128)S(1)} all-reduce(f32[64,64]{1,0:T(8,128)S(1)} %fusion.113), channel_id=1, replica_groups=mesh['cmp'=32,'tgt'=16] {'tgt'}, use_global_device_ids=true, to_apply=%region_22.28 | all-reduce | flops 4096 | bytes 32768 | tf_op jit(solution)/shard_map/psum | solution.py:24
  (136 shorter events, 110.5 us)
Async XLA Ops:
  7.2 0.9 copy-start
  7.2 124.6 %all-reduce.11.cloned.1.call-start = ((), (), s32[]{:S(2)}) async-start(), calls=%async_computation | async-start | bytes 131072 | tf_op jit(solution)/shard_map/psum | solution.py:52
  14.7 1.9 copy-start.1
  16.6 4.5 copy-start.2
  21.1 381.1 %all-reduce.13.cloned.1.call-start = ((), (), s32[]{:S(2)}) async-start(), calls=%async_computation.1 | async-start | bytes 131072 | tf_op jit(solution)/shard_map/psum | solution.py:52
  277.3 395.6 %all-reduce.15.cloned.1.call-start = ((), (), s32[]{:S(2)}) async-start(), calls=%async_computation.2 | async-start | bytes 131072 | tf_op jit(solution)/shard_map/psum | solution.py:52
  547.7 395.9 %all-reduce.17.cloned.1.call-start = ((), (), s32[]{:S(2)}) async-start(), calls=%async_computation.3 | async-start | bytes 131072 | tf_op jit(solution)/shard_map/psum | solution.py:52
  818.7 395.5 %all-reduce.19.cloned.1.call-start = ((), (), s32[]{:S(2)}) async-start(), calls=%async_computation.4 | async-start | bytes 131072 | tf_op jit(solution)/shard_map/psum | solution.py:52
Sparse Core Ops, SparseCore 0:
  21.2 110.5 all-reduce.10
  277.4 124.7 all-reduce.12
  547.9 124.9 all-reduce.14
  818.8 124.8 all-reduce.16
  1089.3 124.8 all-reduce.18
where the time goes:
time: 1440 us; the launch traced here: 1430 us
  blocking collectives  982 us (68%)
  waiting for transfers between devices  220 us (15%)
  other arithmetic  122 us (8%)
  matrix products  85.4 us (6%)
  between operations  14.6 us (1%)
    psum x5, blocking collectives, body(): target_sum, compound_gram = lax.psum((second, gram_of(compound_raw)), 'cmp')  582 us
    psum x6, blocking collectives, target_total(): return lax.psum(partial_gram, 'tgt')  400 us
    psum x5, waiting for transfers between devices, body(): summed = lax.psum(first, 'tgt')  219 us
    another operation x30, other arithmetic, solve_normal(): lower = jnp.linalg.cholesky(normal)  65.2 us
    another operation x20, other arithmetic, solve_normal(): lax.linalg.triangular_solve(lower, middle, left_side=False, lower=True, t...  55.5 us
    dot_general x5, matrix products, body(): jnp.einsum('ijr,ir->jr', inner_again, compound_raw, precision=lax.Precisi...  38.5 us
    dot_general x5, matrix products, body(): jnp.einsum('ijr,jr->ir', inner, target_raw, precision=lax.Precision.HIGHEST)  29.6 us
  transfers between devices with their start and end apart: 5, of which 5 were waited for; matrix products, arithmetic and copies ran while one was open for 4% of the time, Pallas kernels for 0%

commit v1 on v0

v1 whole, which is shorter than its diff:
```python
import functools

import jax
import jax.numpy as jnp
from jax import lax
from jax.experimental import pallas as pl
from jax.experimental.pallas import tpu as pltpu
from jax.sharding import PartitionSpec as P

ITERS = 5
RANK = 64
LANES = 128
PIECES = 4
CHUNKS = 8
HIGHEST = lax.Precision.HIGHEST


def dot_f32(a, b, dims=((1,), (0,))):
    return lax.dot_general(
        a, b, (dims, ((), ())), precision=HIGHEST, preferred_element_type=jnp.float32
    )


def tree_sum(parts):
    parts = list(parts)
    while len(parts) > 1:
        merged = [parts[i] + parts[i + 1] for i in range(0, len(parts) - 1, 2)]
        if len(parts) % 2:
            merged.append(parts[-1])
        parts = merged
    return parts[0]


def swap_halves(x):
    return pltpu.roll(x, RANK, 1)


def lane_of(shape):
    return lax.broadcasted_iota(jnp.int32, shape, 1)


def row_of(shape):
    return lax.broadcasted_iota(jnp.int32, shape, 0)


def inverse_of(tiles):
    tiles = list(tiles)
    shape = (8, LANES)
    row = row_of(shape)
    for b in range(8):
        first = 8 * b
        top = tiles[b]
        spread = [jnp.broadcast_to(top[:, first + c : first + c + 1], shape) for c in range(8)]
        for k in range(8):
            scale = 1.0 / jnp.broadcast_to(spread[k][k : k + 1], shape)
            pivot = jnp.broadcast_to(top[k : k + 1], shape) * scale
            top = jnp.where(row == k, pivot, top - spread[k] * pivot)
            for c in range(k + 1, 8):
                entry = jnp.broadcast_to(spread[c][k : k + 1], shape) * scale
                spread[c] = jnp.where(row == k, entry, spread[c] - spread[k] * entry)
        pivots = [jnp.broadcast_to(top[c : c + 1], shape) for c in range(8)]
        for t in range(8):
            if t == b:
                continue
            terms = [
                jnp.broadcast_to(tiles[t][:, first + c : first + c + 1], shape) * pivots[c]
                for c in range(8)
            ]
            tiles[t] = tiles[t] - tree_sum(terms)
        tiles[b] = top
    return jnp.concatenate(tiles, axis=0)


def both_sides(right):
    left = lane_of(right.shape) < RANK
    return jnp.concatenate(
        [jnp.where(left, swap_halves(right), 0.0), jnp.where(left, 0.0, right)], axis=0
    )


class Ring:
    def __init__(self, axis, n, offset, send, recv, total, sems):
        self.axis, self.n = axis, n
        self.stride = {32: 9, 16: 5}.get(n, n // PIECES)
        self.offset = offset
        self.me = lax.axis_index(axis)
        self.send, self.recv, self.total, self.sems = send, recv, total, sems
        self.owns = lax.rem(self.me, self.stride) == offset
        self.piece = lax.div(self.me, self.stride)

    def copy(self, src, dst, peer, phase):
        return pltpu.make_async_remote_copy(
            src_ref=src,
            dst_ref=dst,
            send_sem=self.sems.at[2 * phase],
            recv_sem=self.sems.at[2 * phase + 1],
            device_id={self.axis: peer},
            device_id_type=pl.DeviceIdType.MESH,
        )

    def scatter(self):
        n = self.n
        for p in range(PIECES):
            owner = self.stride * p + self.offset
            slot = lax.rem(self.me - owner + n, n) - 1

            @pl.when(self.me != owner)
            def _():
                self.copy(self.send.at[p], self.recv.at[slot], owner, 0).start()

    def gather(self):
        n = self.n

        @pl.when(self.owns)
        def _():
            self.copy(self.recv, self.recv, 0, 0).wait_recv()
            self.total[self.piece] = tree_sum(
                [self.send[self.piece]] + [self.recv[k] for k in range(n - 1)]
            )

            @pl.loop(1, n)
            def _(k):
                peer = lax.rem(self.me + k, n)
                self.copy(
                    self.total.at[self.piece], self.total.at[self.piece], peer, 1
                ).start()

    def finish(self):
        @pl.when(self.owns)
        def _():
            some = self.total.at[pl.ds(0, PIECES - 1)]
            self.copy(some, some, 0, 1).wait_recv()
            self.copy(some, some, 0, 0).wait_send()
            self.copy(self.recv, self.recv, 0, 1).wait_send()

        @pl.when(jnp.logical_not(self.owns))
        def _():
            self.copy(self.total, self.total, 0, 1).wait_recv()
            self.copy(self.total, self.total, 0, 0).wait_send()

        return self.total[...].reshape(8 * PIECES, LANES)


def kernel(
    n_cmp,
    n_tgt,
    x_hbm,
    init_ref,
    cond_ref,
    compound_out,
    target_out,
    x_ref,
    inner,
    cond_gram,
    raw_ref,
    side_ref,
    tg_send,
    tg_recv,
    tg_total,
    cg_send,
    cg_recv,
    cg_total,
    cs_send,
    cs_recv,
    cs_total,
    f_send,
    f_recv,
    f_total,
    d_send,
    d_recv,
    x_sems,
    tg_sems,
    cg_sems,
    cs_sems,
    f_sems,
    d_sems,
):
    me_c = lax.axis_index("cmp")
    me_t = lax.axis_index("tgt")
    half = inner.shape[0]
    per = half // CHUNKS
    rows = half // n_tgt

    def fetch(c):
        return [
            pltpu.make_async_copy(
                x_hbm.at[pl.ds(h * half + c * per, per)],
                x_ref.at[pl.ds(h * half + c * per, per)],
                x_sems.at[2 * c + h],
            )
            for h in range(2)
        ]

    for c in range(CHUNKS):
        for one in fetch(c):
            one.start()

    barrier = pltpu.get_barrier_semaphore()

    @pl.loop(1, n_cmp)
    def _(k):
        pl.semaphore_signal(
            barrier,
            inc=1,
            device_id={"cmp": lax.rem(me_c + k, n_cmp)},
            device_id_type=pl.DeviceIdType.MESH,
        )

    @pl.loop(1, n_tgt)
    def _(k):
        pl.semaphore_signal(
            barrier,
            inc=1,
            device_id={"tgt": lax.rem(me_t + k, n_tgt)},
            device_id_type=pl.DeviceIdType.MESH,
        )

    full = (RANK, LANES)
    packed = (8 * PIECES, LANES)
    left_full = lane_of(full) < RANK
    left = lane_of(packed) < RANK
    eye = (lane_of(full) == row_of(full) + RANK).astype(jnp.float32)
    pair = jnp.logical_or(lane_of(full) == row_of(full), lane_of(full) == row_of(full) + RANK)
    twice = pair.astype(jnp.bfloat16)

    cond = cond_ref[...]
    cond_twice = lax.dot_general(
        cond, twice, (((0,), (0,)), ((), ())), preferred_element_type=jnp.float32
    )
    cond_gram[...] = lax.dot_general(
        cond_twice.astype(jnp.bfloat16),
        cond_twice.astype(jnp.bfloat16),
        (((0,), (0,)), ((), ())),
        preferred_element_type=jnp.float32,
    )[:RANK]
    wide_left = lane_of(cond_twice.shape) < RANK
    weights = jnp.concatenate(
        [jnp.where(wide_left, cond_twice, 0.0), jnp.where(wide_left, 0.0, cond_twice)], axis=0
    ).astype(jnp.bfloat16)

    for c in range(CHUNKS):
        for one in fetch(c):
            one.wait()

        @pl.loop(0, per // 8)
        def _(s):
            at = c * per + s * 8
            block = jnp.concatenate([x_ref[pl.ds(at, 8)], x_ref[pl.ds(half + at, 8)]], axis=2)
            flat = block.reshape(8 * RANK, 2 * LANES)
            made = jnp.dot(flat, weights, preferred_element_type=jnp.float32)
            inner[pl.ds(at, 8)] = made.reshape(8, RANK, LANES)

    tg = Ring("tgt", n_tgt, 0, tg_send, tg_recv, tg_total, tg_sems)
    cg = Ring("cmp", n_cmp, 0, cg_send, cg_recv, cg_total, cg_sems)
    cs_offset = {32: 4}.get(n_cmp, 1)
    cs = Ring("cmp", n_cmp, cs_offset, cs_send, cs_recv, cs_total, cs_sems)

    def f_copy(src, dst, peer, phase):
        return pltpu.make_async_remote_copy(
            src_ref=src,
            dst_ref=dst,
            send_sem=f_sems.at[2 * phase],
            recv_sem=f_sems.at[2 * phase + 1],
            device_id={"tgt": peer},
            device_id_type=pl.DeviceIdType.MESH,
        )

    def normal_inverse(total):
        whole = jnp.concatenate([total, swap_halves(total)], axis=0)
        whole = jnp.where(left_full, whole * cond_gram[...], eye)
        return both_sides(inverse_of([whole[8 * t : 8 * t + 8] for t in range(8)]))

    side_ref[...] = jnp.dot(init_ref[...], twice, preferred_element_type=jnp.float32)
    pl.semaphore_wait(barrier, n_cmp + n_tgt - 2)

    @pl.loop(0, ITERS)
    def _(sweep):
        target = side_ref[...]
        square = dot_f32(target, target, ((0,), (0,)))
        tg_send[...] = jnp.where(left, square[:32], square[32:64]).reshape(tg_send.shape)
        tg.scatter()

        def block_of(owner):
            sums = []
            for s in range(0, rows, 8):
                part = inner[pl.ds(owner * rows + s, 8)]
                sums.append(jnp.sum(part * target[None], axis=1))
            return jnp.concatenate(sums, axis=0) if len(sums) > 1 else sums[0]

        @pl.loop(1, n_tgt)
        def _(k):
            peer = lax.rem(me_t + k, n_tgt)
            f_send[peer] = block_of(peer)
            f_copy(f_send.at[peer], f_recv.at[k - 1], peer, 0).start()

        mine = block_of(me_t)
        tg.gather()
        f_copy(f_recv, f_recv, 0, 0).wait_recv()
        f_total[me_t] = tree_sum([mine] + [f_recv[k] for k in range(n_tgt - 1)])

        @pl.loop(1, n_tgt)
        def _(k):
            peer = lax.rem(me_t + k, n_tgt)
            f_copy(f_total.at[me_t], f_total.at[me_t], peer, 1).start()

        across = normal_inverse(tg.finish())
        f_copy(f_recv, f_recv, 0, 0).wait_send()
        f_copy(f_recv, f_recv, 0, 1).wait()
        compound = dot_f32(f_total[...].reshape(half, LANES), across)
        raw_ref[...] = compound

        square = dot_f32(compound, compound, ((0,), (0,)))
        low = square[:32] + swap_halves(square[64:96])
        high = swap_halves(square[32:64]) + square[96:128]
        cg_send[...] = jnp.where(left, low, high).reshape(cg_send.shape)
        cg.scatter()

        def add_rows(s, sums):
            sums = list(sums)
            for d in range(8):
                at = s * 8 + d
                line = jnp.broadcast_to(raw_ref[pl.ds(at, 1), :], (8, LANES))
                for t in range(8):
                    sums[t] = sums[t] + inner[at, 8 * t : 8 * t + 8, :] * line
            return tuple(sums)

        zero = jnp.zeros((8, LANES), jnp.float32)
        sums = lax.fori_loop(0, half // 8, add_rows, (zero,) * 8)
        for p in range(PIECES):
            top = sums[p] + swap_halves(sums[p])
            bottom = sums[p + 4] + swap_halves(sums[p + 4])
            cs_send[p] = jnp.where(left[:8], top, bottom)
        cs.scatter()
        cg.gather()
        cs.gather()
        across = normal_inverse(cg.finish())
        both = dot_f32(cs.finish(), across)
        other = swap_halves(both)
        side_ref[...] = jnp.concatenate(
            [jnp.where(left, both, other), jnp.where(left, other, both)], axis=0
        )

    target = side_ref[...]
    d_send[...] = tree_sum([target[8 * t : 8 * t + 8] * target[8 * t : 8 * t + 8] for t in range(8)])

    def d_copy(src, dst, peer):
        return pltpu.make_async_remote_copy(
            src_ref=src,
            dst_ref=dst,
            send_sem=d_sems.at[0],
            recv_sem=d_sems.at[1],
            device_id={"tgt": peer},
            device_id_type=pl.DeviceIdType.MESH,
        )

    @pl.loop(1, n_tgt)
    def _(k):
        d_copy(d_send, d_recv.at[k - 1], lax.rem(me_t + k, n_tgt)).start()

    total = cg_total[...].reshape(packed)
    other = swap_halves(total)
    whole = jnp.concatenate([jnp.where(left, total, other), jnp.where(left, other, total)], axis=0)
    diagonal = jnp.sum(jnp.where(pair, whole, 0.0), axis=0, keepdims=True)
    compound_count = 2 * half * n_cmp
    scaled = (raw_ref[...] / jnp.sqrt(diagonal / compound_count + 1e-06)).T
    compound_out[:, :half] = scaled[:RANK]
    compound_out[:, half:] = scaled[RANK:]

    d_copy(d_recv, d_recv, 0).wait()
    squares = tree_sum([d_send[...]] + [d_recv[k] for k in range(n_tgt - 1)])
    diagonal = jnp.sum(squares, axis=0, keepdims=True)
    target_count = RANK * n_tgt
    scaled = target / jnp.sqrt(diagonal / target_count + 1e-06)
    target_out[...] = scaled[:, :RANK]


def body(n_cmp, n_tgt, responses, target_init, condition_factor):
    cmp_rows, tgt_rows, cond_count = responses.shape
    half = cmp_rows // 2
    rows = half // n_tgt
    vmem = pltpu.VMEM
    f32 = jnp.float32

    def ring(n):
        return [vmem((PIECES, 8, LANES), f32), vmem((n - 1, 8, LANES), f32), vmem((PIECES, 8, LANES), f32)]

    compound, target = pl.pallas_call(
        functools.partial(kernel, n_cmp, n_tgt),
        out_shape=(
            jax.ShapeDtypeStruct((RANK, cmp_rows), f32),
            jax.ShapeDtypeStruct((tgt_rows, RANK), f32),
        ),
        in_specs=[
            pl.BlockSpec(memory_space=pl.ANY),
            pl.BlockSpec(memory_space=vmem),
            pl.BlockSpec(memory_space=vmem),
        ],
        out_specs=(pl.BlockSpec(memory_space=vmem), pl.BlockSpec(memory_space=vmem)),
        scratch_shapes=[
            vmem((cmp_rows, tgt_rows, cond_count), jnp.bfloat16),
            vmem((half, tgt_rows, LANES), f32),
            vmem((RANK, LANES), f32),
            vmem((half, LANES), f32),
            vmem((tgt_rows, LANES), f32),
            *ring(n_tgt),
            *ring(n_cmp),
            *ring(n_cmp),
            vmem((n_tgt, rows, LANES), f32),
            vmem((n_tgt - 1, rows, LANES), f32),
            vmem((n_tgt, rows, LANES), f32),
            vmem((8, LANES), f32),
            vmem((n_tgt - 1, 8, LANES), f32),
            pltpu.SemaphoreType.DMA((2 * CHUNKS,)),
            pltpu.SemaphoreType.DMA((4,)),
            pltpu.SemaphoreType.DMA((4,)),
            pltpu.SemaphoreType.DMA((4,)),
            pltpu.SemaphoreType.DMA((4,)),
            pltpu.SemaphoreType.DMA((2,)),
        ],
        compiler_params=pltpu.CompilerParams(
            collective_id=0, has_side_effects=True, vmem_limit_bytes=48 * 1024 * 1024
        ),
        cost_estimate=pl.CostEstimate(
            flops=2 * cmp_rows * tgt_rows * RANK * (cond_count + 2 * ITERS),
            bytes_accessed=2 * cmp_rows * tgt_rows * cond_count,
            transcendentals=0,
        ),
    )(responses, target_init, condition_factor.T)
    return compound.T, target


def solution(mesh):
    return jax.shard_map(
        functools.partial(body, mesh.shape["cmp"], mesh.shape["tgt"]),
        mesh=mesh,
        in_specs=(P("cmp", "tgt", None), P("tgt", None), P()),
        out_specs=(P("cmp", None), P("tgt", None)),
        check_vma=False,
    )
```

time: 1440 us -> 163 us (0.11)
  blocking collectives: 982 us -> 0 us
  waiting for transfers between devices: 220 us -> 0 us
  Pallas kernels: 0 us -> 157 us
  other arithmetic: 122 us -> 0 us
  matrix products: 85.4 us -> 0 us
    psum x11 -> x0, blocking collectives: 982 us -> none  [the longest x5 582 us: body(): target_sum, compound_gram = lax.psum((second, gram_of(compound_raw)), 'cmp')]
    psum x5 -> x0, waiting for transfers between devices: 219 us -> none  [body(): summed = lax.psum(first, 'tgt')]
    pallas_call x0 -> x1, Pallas kernels: none -> 157 us  [body(): pl.pallas_call(functools.partial(kernel, n_cmp, n_tgt), out_shape=(jax.Sh...]
    another operation x50 -> x0, other arithmetic: 121 us -> none  [the longest x30 65.2 us: solve_normal(): lower = jnp.linalg.cholesky(normal)]
    dot_general x23 -> x0, matrix products: 76.9 us -> none  [the longest x5 38.5 us: body(): jnp.einsum('ijr,ir->jr', inner_again, compound_raw, precision=lax.Precisi...]
  transfers between devices with their start and end apart: 5 -> 0, of which waited for: 5 -> 0; matrix products, arithmetic and copies ran while one was open for 4% -> 0% of each run, Pallas kernels for 0% -> 0%
where the time goes in v1:
time: 163 us; the launch traced here: 162 us
  Pallas kernels  157 us (96%)
  local copies, waits for them, and re-layouts  4.86 us (3%)
    pallas_call x1, Pallas kernels, body(): pl.pallas_call(functools.partial(kernel, n_cmp, n_tgt), out_shape=(jax.Sh...  157 us
    unnamed x8, local copies, waits for them, and re-layouts  4.86 us

profile of v1, /device:TPU:1, one launch (start us, length us, event | category | flops | bytes accessed | tf_op | source)
XLA Modules:
  0.0 162.5 jit_solution(4798363055229479505)
XLA Ops:
  0.6 0.0 copy-start
  0.6 2.2 %copy-done = bf16[256,64,128]{2,1,0:T(8,128)(2,1)S(1)} copy-done((bf16[256,64,128]{2,1,0:T(8,128)(2,1)S(1)}, bf16[256,64,128]{2,1,0:T(8,128)(2,1)}, u32[]{:S(2)}) %copy-start) | copy-done | bytes 4194328
  2.8 0.0 copy-start.1
  2.8 0.7 copy-done.1
  3.5 0.0 copy-start.2
  3.5 0.7 copy-done.2
  4.3 156.9 %shard_map.50 = (f32[64,256]{1,0:T(8,128)S(1)}, f32[64,64]{1,0:T(8,128)S(1)}) custom-call(bf16[256,64,128]{2,1,0:T(8,128)(2,1)S(1)} %copy-done, bf16[64,64]{1,0:T(8,128)(2,1)S(1)} %copy-done.1, bf16[64,128]{1,0:T(8,128)(2,1)S(1)} %bitcast.3), custom_call_target="tpu_custom_call" | custom-call | flops 289406976 | bytes 4194304 | tf_op jit(solution)/shard_map/pallas_call | solution.py:387
  161.2 0.6 copy.7
  161.8 0.6 copy.8
Async XLA Ops:
  0.6 2.2 %copy-start = (bf16[256,64,128]{2,1,0:T(8,128)(2,1)S(1)}, bf16[256,64,128]{2,1,0:T(8,128)(2,1)}, u32[]{:S(2)}) copy-start(bf16[256,64,128]{2,1,0:T(8,128)(2,1)} %x_hbm.1) | copy-start | bytes 12582916
  2.8 0.7 copy-start.1
  3.5 0.7 copy-start.2

commit v2 on v1

v2 whole, which is shorter than its diff:
```python
import functools

import jax
import jax.numpy as jnp
from jax import lax
from jax.experimental import pallas as pl
from jax.experimental.pallas import tpu as pltpu
from jax.sharding import PartitionSpec as P

ITERS = 5
RANK = 64
LANES = 128
PIECES = 4
CHUNKS = 8
HIGHEST = lax.Precision.HIGHEST


def dot_f32(a, b, dims=((1,), (0,))):
    return lax.dot_general(
        a, b, (dims, ((), ())), precision=HIGHEST, preferred_element_type=jnp.float32
    )


def tree_sum(parts):
    parts = list(parts)
    while len(parts) > 1:
        merged = [parts[i] + parts[i + 1] for i in range(0, len(parts) - 1, 2)]
        if len(parts) % 2:
            merged.append(parts[-1])
        parts = merged
    return parts[0]


def swap_halves(x):
    return pltpu.roll(x, RANK, 1)


def lane_of(shape):
    return lax.broadcasted_iota(jnp.int32, shape, 1)


def row_of(shape):
    return lax.broadcasted_iota(jnp.int32, shape, 0)


def inverse_of(tiles):
    tiles = list(tiles)
    shape = (8, LANES)
    row = row_of(shape)
    for b in range(8):
        first = 8 * b
        top = tiles[b]
        spread = [jnp.broadcast_to(top[:, first + c : first + c + 1], shape) for c in range(8)]
        for k in range(8):
            scale = 1.0 / jnp.broadcast_to(spread[k][k : k + 1], shape)
            pivot = jnp.broadcast_to(top[k : k + 1], shape) * scale
            top = jnp.where(row == k, pivot, top - spread[k] * pivot)
            for c in range(k + 1, 8):
                entry = jnp.broadcast_to(spread[c][k : k + 1], shape) * scale
                spread[c] = jnp.where(row == k, entry, spread[c] - spread[k] * entry)
        pivots = [jnp.broadcast_to(top[c : c + 1], shape) for c in range(8)]
        for t in range(8):
            if t == b:
                continue
            terms = [
                jnp.broadcast_to(tiles[t][:, first + c : first + c + 1], shape) * pivots[c]
                for c in range(8)
            ]
            tiles[t] = tiles[t] - tree_sum(terms)
        tiles[b] = top
    return jnp.concatenate(tiles, axis=0)


def both_sides(right):
    left = lane_of(right.shape) < RANK
    return jnp.concatenate(
        [jnp.where(left, swap_halves(right), 0.0), jnp.where(left, 0.0, right)], axis=0
    )


def ring_offsets(outer, inner):
    pairs = [(a, b) for a in range(outer) for b in range(inner) if a or b]
    return sorted(pairs, key=lambda p: -(min(p[0], outer - p[0]) + min(p[1], inner - p[1])))


def peer_at(me, offset, outer, inner):
    a = lax.rem(lax.div(me, inner) + offset[0], outer)
    b = lax.rem(lax.rem(me, inner) + offset[1], inner)
    return a * inner + b


def kernel(
    n_cmp,
    n_tgt,
    x_hbm,
    init_hbm,
    cond_hbm,
    compound_out,
    target_out,
    x_ref,
    init_ref,
    cond_ref,
    inner,
    cond_gram,
    raw_ref,
    side_ref,
    tg_part,
    tg_core,
    tg_line,
    tg_total,
    cg_part,
    cg_plane,
    cg_total,
    cs_send,
    cs_recv,
    cs_plane,
    f_send,
    f_recv,
    f_total,
    d_send,
    d_recv,
    x_sems,
    send_sems,
    recv_sems,
    line_sems,
    cg_sems,
    cs_sems,
):
    me_c = lax.axis_index("cmp")
    me_t = lax.axis_index("tgt")
    n_x, n_z = PIECES, n_cmp // PIECES
    n_y = n_tgt // 2
    me_x = lax.rem(me_c, n_x)
    me_y, core = lax.div(me_t, 2), lax.rem(me_t, 2)
    mate = 2 * me_y + 1 - core
    half = inner.shape[0]
    per = half // CHUNKS
    rows = half // n_tgt
    plane = ring_offsets(n_z, n_x)
    line = ring_offsets(n_y, 2)

    def fetch(c):
        return [
            pltpu.make_async_copy(
                x_hbm.at[pl.ds(h * half + c * per, per)],
                x_ref.at[pl.ds(h * half + c * per, per)],
                x_sems.at[2 * c + h],
            )
            for h in range(2)
        ]

    small = [
        pltpu.make_async_copy(cond_hbm, cond_ref, x_sems.at[2 * CHUNKS]),
        pltpu.make_async_copy(init_hbm, init_ref, x_sems.at[2 * CHUNKS + 1]),
    ]
    for one in small:
        one.start()
    for c in range(CHUNKS):
        for one in fetch(c):
            one.start()

    barrier = pltpu.get_barrier_semaphore()
    for offset in plane:
        pl.semaphore_signal(
            barrier,
            inc=1,
            device_id={"cmp": peer_at(me_c, offset, n_z, n_x)},
            device_id_type=pl.DeviceIdType.MESH,
        )
    for offset in line:
        pl.semaphore_signal(
            barrier,
            inc=1,
            device_id={"tgt": peer_at(me_t, offset, n_y, 2)},
            device_id_type=pl.DeviceIdType.MESH,
        )

    def remote(src, dst, send_sem, recv_sem, axis, peer):
        return pltpu.make_async_remote_copy(
            src_ref=src,
            dst_ref=dst,
            send_sem=send_sems.at[send_sem],
            recv_sem=recv_sem,
            device_id={axis: peer},
            device_id_type=pl.DeviceIdType.MESH,
        )

    full = (RANK, LANES)
    packed = (8 * PIECES, LANES)
    left_full = lane_of(full) < RANK
    left = lane_of(packed) < RANK
    eye = (lane_of(full) == row_of(full) + RANK).astype(jnp.float32)
    pair = jnp.logical_or(lane_of(full) == row_of(full), lane_of(full) == row_of(full) + RANK)
    twice = pair.astype(jnp.bfloat16)

    for one in small:
        one.wait()
    cond = cond_ref[...]
    cond_twice = lax.dot_general(
        cond, twice, (((0,), (0,)), ((), ())), preferred_element_type=jnp.float32
    )
    cond_gram[...] = lax.dot_general(
        cond_twice.astype(jnp.bfloat16),
        cond_twice.astype(jnp.bfloat16),
        (((0,), (0,)), ((), ())),
        preferred_element_type=jnp.float32,
    )[:RANK]
    wide_left = lane_of(cond_twice.shape) < RANK
    weights = jnp.concatenate(
        [jnp.where(wide_left, cond_twice, 0.0), jnp.where(wide_left, 0.0, cond_twice)], axis=0
    ).astype(jnp.bfloat16)
    side_ref[...] = jnp.dot(init_ref[...], twice, preferred_element_type=jnp.float32)

    for c in range(CHUNKS):
        for one in fetch(c):
            one.wait()

        @pl.loop(0, per // 8)
        def _(s):
            at = c * per + s * 8
            block = jnp.concatenate([x_ref[pl.ds(at, 8)], x_ref[pl.ds(half + at, 8)]], axis=2)
            flat = block.reshape(8 * RANK, 2 * LANES)
            made = jnp.dot(flat, weights, preferred_element_type=jnp.float32)
            inner[pl.ds(at, 8)] = made.reshape(8, RANK, LANES)

    def normal_inverse(total):
        whole = jnp.concatenate([total, swap_halves(total)], axis=0)
        whole = jnp.where(left_full, whole * cond_gram[...], eye)
        return both_sides(inverse_of([whole[8 * t : 8 * t + 8] for t in range(8)]))

    def swap_cores(total, index):
        copy = remote(total.at[core], total.at[core], index, recv_sems.at[index], "tgt", mate)
        copy.start()
        return copy

    pl.semaphore_wait(barrier, n_cmp + n_tgt - 2)

    @pl.loop(0, ITERS)
    def _(sweep):
        turn = lax.rem(sweep, 2)

        target = side_ref[...]

        def block_of(owner):
            sums = []
            for s in range(0, rows, 8):
                part = inner[pl.ds(owner * rows + s, 8)]
                sums.append(jnp.sum(part * target[None], axis=1))
            return jnp.concatenate(sums, axis=0) if len(sums) > 1 else sums[0]

        def f_copy(src, dst, phase, peer):
            return remote(src, dst, phase, recv_sems.at[phase], "tgt", peer)

        for offset in line:
            peer = peer_at(me_t, offset, n_y, 2)
            slot = lax.rem(me_t - peer + n_tgt, n_tgt) - 1
            f_send[peer] = block_of(peer)
            f_copy(f_send.at[peer], f_recv.at[slot], 0, peer).start()

        square = dot_f32(target, target, ((0,), (0,)))
        tg_part[...] = jnp.where(left, square[:32], square[32:64]).reshape(tg_part.shape)
        to_mate = remote(tg_part.at[1 - core], tg_core, 2, recv_sems.at[2], "tgt", mate)
        to_mate.start()
        mine = block_of(me_t)
        to_mate.wait_recv()
        tg_line[turn, me_y] = tg_part[core] + tg_core[...]
        own = tg_line.at[turn, me_y]
        for offset in line:
            if offset[1] == 0:
                peer = peer_at(me_t, offset, n_y, 2)
                remote(own, own, 3, line_sems.at[turn], "tgt", peer).start()

        f_copy(f_recv, f_recv, 0, mate).wait_recv()
        f_total[me_t] = tree_sum([mine] + [f_recv[k] for k in range(n_tgt - 1)])
        for offset in line:
            peer = peer_at(me_t, offset, n_y, 2)
            f_copy(f_total.at[me_t], f_total.at[me_t], 1, peer).start()

        others = tg_line.at[turn, pl.ds(0, n_y - 1)]
        remote(others, others, 3, line_sems.at[turn], "tgt", mate).wait_recv()
        tg_total[core] = tree_sum([tg_line[turn, k] for k in range(n_y)])
        swap = swap_cores(tg_total, 4)
        swap.wait_recv()
        across = normal_inverse(tg_total[...].reshape(packed))
        f_copy(f_recv, f_recv, 1, mate).wait_recv()
        compound = dot_f32(f_total[...].reshape(half, LANES), across)
        raw_ref[...] = compound

        def add_rows(s, sums):
            sums = list(sums)
            for d in range(8):
                at = s * 8 + d
                spread = jnp.broadcast_to(raw_ref[pl.ds(at, 1), :], (8, LANES))
                for t in range(8):
                    sums[t] = sums[t] + inner[at, 8 * t : 8 * t + 8, :] * spread
            return tuple(sums)

        zero = jnp.zeros((8, LANES), jnp.float32)
        sums = lax.fori_loop(0, half // 8, add_rows, (zero,) * 8)
        for p in range(PIECES):
            top = sums[p] + swap_halves(sums[p])
            bottom = sums[p + 4] + swap_halves(sums[p + 4])
            cs_send[p] = jnp.where(left[:8], top, bottom)
        for d in (2, 1, 3):
            x = lax.rem(me_x + d, n_x)
            peer = me_c - me_x + x
            remote(cs_send.at[x], cs_recv.at[d - 1], 5, recv_sems.at[5], "cmp", peer).start()

        square = dot_f32(compound, compound, ((0,), (0,)))
        low = square[:32] + swap_halves(square[64:96])
        high = swap_halves(square[32:64]) + square[96:128]
        cg_part[...] = jnp.where(left, low, high).reshape(cg_part.shape)
        cg_plane[turn, me_c] = cg_part[core]
        own = cg_plane.at[turn, me_c]
        for offset in plane:
            peer = peer_at(me_c, offset, n_z, n_x)
            remote(own, own, 6, cg_sems.at[turn], "cmp", peer).start()

        remote(cs_recv, cs_recv, 5, recv_sems.at[5], "cmp", me_c).wait_recv()
        cs_plane[turn, me_c] = (cs_send[me_x] + cs_recv[0]) + (cs_recv[1] + cs_recv[2])
        own = cs_plane.at[turn, me_c]
        for offset in plane:
            peer = peer_at(me_c, offset, n_z, n_x)
            remote(own, own, 7, cs_sems.at[turn], "cmp", peer).start()

        others = cg_plane.at[turn, pl.ds(0, n_cmp - 1)]
        cg_all = remote(others, others, 6, cg_sems.at[turn], "cmp", me_c)
        cg_all.wait_recv()
        cg_total[core] = tree_sum([cg_plane[turn, k] for k in range(n_cmp)])
        swap_c = swap_cores(cg_total, 8)
        swap_c.wait_recv()
        across = normal_inverse(cg_total[...].reshape(packed))
        others = cs_plane.at[turn, pl.ds(0, n_cmp - 1)]
        cs_all = remote(others, others, 7, cs_sems.at[turn], "cmp", me_c)
        cs_all.wait_recv()
        pieces = [
            tree_sum([cs_plane[turn, z * n_x + p] for z in range(n_z)]) for p in range(PIECES)
        ]
        both = dot_f32(jnp.concatenate(pieces, axis=0), across)
        other = swap_halves(both)
        side_ref[...] = jnp.concatenate(
            [jnp.where(left, both, other), jnp.where(left, other, both)], axis=0
        )

        f_copy(f_recv, f_recv, 0, mate).wait_send()
        f_copy(f_recv, f_recv, 1, mate).wait_send()
        to_mate.wait_send()
        others = tg_line.at[turn, pl.ds(0, n_y - 1)]
        remote(others, others, 3, line_sems.at[turn], "tgt", mate).wait_send()
        swap.wait_send()
        remote(cs_recv, cs_recv, 5, recv_sems.at[5], "cmp", me_c).wait_send()
        cg_all.wait_send()
        cs_all.wait_send()
        swap_c.wait_send()

    target = side_ref[...]
    d_send[...] = tree_sum([target[8 * t : 8 * t + 8] * target[8 * t : 8 * t + 8] for t in range(8)])
    for offset in line:
        peer = peer_at(me_t, offset, n_y, 2)
        slot = lax.rem(me_t - peer + n_tgt, n_tgt) - 1
        remote(d_send, d_recv.at[slot], 9, recv_sems.at[9], "tgt", peer).start()

    total = cg_total[...].reshape(packed)
    other = swap_halves(total)
    whole = jnp.concatenate([jnp.where(left, total, other), jnp.where(left, other, total)], axis=0)
    diagonal = jnp.sum(jnp.where(pair, whole, 0.0), axis=0, keepdims=True)
    compound_count = 2 * half * n_cmp
    scaled = (raw_ref[...] / jnp.sqrt(diagonal / compound_count + 1e-06)).T
    compound_out[:, :half] = scaled[:RANK]
    compound_out[:, half:] = scaled[RANK:]

    remote(d_recv, d_recv, 9, recv_sems.at[9], "tgt", mate).wait()
    squares = tree_sum([d_send[...]] + [d_recv[k] for k in range(n_tgt - 1)])
    diagonal = jnp.sum(squares, axis=0, keepdims=True)
    target_count = RANK * n_tgt
    scaled = target / jnp.sqrt(diagonal / target_count + 1e-06)
    target_out[...] = scaled[:, :RANK]


def body(n_cmp, n_tgt, responses, target_init, condition_factor):
    cmp_rows, tgt_rows, cond_count = responses.shape
    half = cmp_rows // 2
    rows = half // n_tgt
    vmem = pltpu.VMEM
    f32 = jnp.float32

    compound, target = pl.pallas_call(
        functools.partial(kernel, n_cmp, n_tgt),
        out_shape=(
            jax.ShapeDtypeStruct((RANK, cmp_rows), f32),
            jax.ShapeDtypeStruct((tgt_rows, RANK), f32),
        ),
        in_specs=[pl.BlockSpec(memory_space=pltpu.HBM)] * 3,
        out_specs=(pl.BlockSpec(memory_space=vmem), pl.BlockSpec(memory_space=vmem)),
        scratch_shapes=[
            vmem((cmp_rows, tgt_rows, cond_count), jnp.bfloat16),
            vmem(target_init.shape, jnp.bfloat16),
            vmem((RANK, cond_count), jnp.bfloat16),
            vmem((half, tgt_rows, LANES), f32),
            vmem((RANK, LANES), f32),
            vmem((half, LANES), f32),
            vmem((tgt_rows, LANES), f32),
            vmem((2, 16, LANES), f32),
            vmem((16, LANES), f32),
            vmem((2, n_tgt // 2, 16, LANES), f32),
            vmem((2, 16, LANES), f32),
            vmem((2, 16, LANES), f32),
            vmem((2, n_cmp, 16, LANES), f32),
            vmem((2, 16, LANES), f32),
            vmem((PIECES, 8, LANES), f32),
            vmem((PIECES - 1, 8, LANES), f32),
            vmem((2, n_cmp, 8, LANES), f32),
            vmem((n_tgt, rows, LANES), f32),
            vmem((n_tgt - 1, rows, LANES), f32),
            vmem((n_tgt, rows, LANES), f32),
            vmem((8, LANES), f32),
            vmem((n_tgt - 1, 8, LANES), f32),
            pltpu.SemaphoreType.DMA((2 * CHUNKS + 2,)),
            pltpu.SemaphoreType.DMA((10,)),
            pltpu.SemaphoreType.DMA((10,)),
            pltpu.SemaphoreType.DMA((2,)),
            pltpu.SemaphoreType.DMA((2,)),
            pltpu.SemaphoreType.DMA((2,)),
        ],
        compiler_params=pltpu.CompilerParams(
            collective_id=0, has_side_effects=True, vmem_limit_bytes=62 * 1024 * 1024
        ),
        cost_estimate=pl.CostEstimate(
            flops=2 * cmp_rows * tgt_rows * RANK * (cond_count + 2 * ITERS),
            bytes_accessed=2 * cmp_rows * tgt_rows * cond_count,
            transcendentals=0,
        ),
    )(responses, target_init, condition_factor.T)
    return compound.T, target


def solution(mesh):
    return jax.shard_map(
        functools.partial(body, mesh.shape["cmp"], mesh.shape["tgt"]),
        mesh=mesh,
        in_specs=(P("cmp", "tgt", None), P("tgt", None), P()),
        out_specs=(P("cmp", None), P("tgt", None)),
        check_vma=False,
    )
```

time: 163 us -> 139 us (0.85)
  Pallas kernels: 157 us -> 136 us
  local copies, waits for them, and re-layouts: 4.86 us -> 2.85 us
    pallas_call x1, Pallas kernels: 157 us -> 136 us  [body(): pl.pallas_call(functools.partial(kernel, n_cmp, n_tgt), out_shape=(jax.Sh...]
    unnamed x8 -> x2, local copies, waits for them, and re-layouts: 4.86 us -> 2.85 us
where the time goes in v2:
time: 139 us
  Pallas kernels  136 us (98%)
  local copies, waits for them, and re-layouts  2.85 us (2%)
    pallas_call x1, Pallas kernels, body(): pl.pallas_call(functools.partial(kernel, n_cmp, n_tgt), out_shape=(jax.Sh...  136 us
    unnamed x2, local copies, waits for them, and re-layouts  2.85 us

profile of v2, /device:TPU:1, one launch (start us, length us, event | category | flops | bytes accessed | tf_op | source)
XLA Modules:
  0.0 139.2 jit_solution(3361965171892907184)
XLA Ops:
  0.6 135.7 %shard_map.50 = (f32[64,256]{1,0:T(8,128)}, f32[64,64]{1,0:T(8,128)}) custom-call(bf16[256,64,128]{2,1,0:T(8,128)(2,1)} %x_hbm.1, bf16[64,64]{1,0:T(8,128)(2,1)} %init_hbm.1, bf16[64,128]{1,0:T(8,128)(2,1)} %bitcast.3), custom_call_target="tpu_custom_call" | custom-call | flops 289406976 | bytes 4194304 | tf_op jit(solution)/shard_map/pallas_call | solution.py:387
  136.3 1.5 %copy.7 = f32[256,64]{0,1:T(8,128)} copy(f32[256,64]{0,1:T(8,128)} %bitcast.2) | data formatting | bytes 131072
  137.8 1.4 copy.8

commit v3 on v2

--- a/solution.py
+++ b/solution.py
@@ -111,6 +111,7 @@
     cg_part,
     cg_plane,
     cg_total,
+    gram_ref,
     cs_send,
     cs_recv,
     cs_plane,
@@ -188,7 +189,8 @@
     full = (RANK, LANES)
     packed = (8 * PIECES, LANES)
     left_full = lane_of(full) < RANK
-    left = lane_of(packed) < RANK
+    lane, row = lane_of(packed), row_of(packed)
+    left = lane < RANK
     eye = (lane_of(full) == row_of(full) + RANK).astype(jnp.float32)
     pair = jnp.logical_or(lane_of(full) == row_of(full), lane_of(full) == row_of(full) + RANK)
     twice = pair.astype(jnp.bfloat16)
@@ -223,9 +225,8 @@
             made = jnp.dot(flat, weights, preferred_element_type=jnp.float32)
             inner[pl.ds(at, 8)] = made.reshape(8, RANK, LANES)
 
-    def normal_inverse(total):
-        whole = jnp.concatenate([total, swap_halves(total)], axis=0)
-        whole = jnp.where(left_full, whole * cond_gram[...], eye)
+    def normal_inverse(gram):
+        whole = jnp.where(left_full, gram * cond_gram[...], eye)
         return both_sides(inverse_of([whole[8 * t : 8 * t + 8] for t in range(8)]))
 
     def swap_cores(total, index):
@@ -281,7 +282,8 @@
         tg_total[core] = tree_sum([tg_line[turn, k] for k in range(n_y)])
         swap = swap_cores(tg_total, 4)
         swap.wait_recv()
-        across = normal_inverse(tg_total[...].reshape(packed))
+        total = tg_total[...].reshape(packed)
+        across = normal_inverse(jnp.concatenate([total, swap_halves(total)], axis=0))
         f_copy(f_recv, f_recv, 1, mate).wait_recv()
         compound = dot_f32(f_total[...].reshape(half, LANES), across)
         raw_ref[...] = compound
@@ -307,11 +309,16 @@
             remote(cs_send.at[x], cs_recv.at[d - 1], 5, recv_sems.at[5], "cmp", peer).start()
 
         square = dot_f32(compound, compound, ((0,), (0,)))
-        low = square[:32] + swap_halves(square[64:96])
-        high = swap_halves(square[32:64]) + square[96:128]
-        cg_part[...] = jnp.where(left, low, high).reshape(cg_part.shape)
-        cg_plane[turn, me_c] = cg_part[core]
-        own = cg_plane.at[turn, me_c]
+        upper = square[:32] + swap_halves(square[64:96])
+        lower = pltpu.roll(square[32:64], 96, 1) + pltpu.roll(square[96:128], 32, 1)
+        triangles = jnp.where(jnp.logical_and(lane < row, lane < 32), lower, upper)
+        folded = jnp.where(left[:16], triangles[:16], swap_halves(triangles[16:]))
+        tail = jnp.sum(jnp.where(lane == row, lower, 0.0), axis=0, keepdims=True)
+        cg_part[0] = folded[:8]
+        cg_part[1] = folded[8:]
+        cg_plane[turn, me_c, :8] = cg_part[core]
+        cg_plane[turn, me_c, 8:9] = tail
+        own = cg_plane.at[turn, me_c, pl.ds(0, 9)]
         for offset in plane:
             peer = peer_at(me_c, offset, n_z, n_x)
             remote(own, own, 6, cg_sems.at[turn], "cmp", peer).start()
@@ -323,13 +330,25 @@
             peer = peer_at(me_c, offset, n_z, n_x)
             remote(own, own, 7, cs_sems.at[turn], "cmp", peer).start()
 
-        others = cg_plane.at[turn, pl.ds(0, n_cmp - 1)]
+        others = cg_plane.at[turn, pl.ds(0, n_cmp - 1), pl.ds(0, 9)]
         cg_all = remote(others, others, 6, cg_sems.at[turn], "cmp", me_c)
         cg_all.wait_recv()
-        cg_total[core] = tree_sum([cg_plane[turn, k] for k in range(n_cmp)])
+        cg_total[core] = tree_sum([cg_plane[turn, k, :8] for k in range(n_cmp)])
         swap_c = swap_cores(cg_total, 8)
+        tail = tree_sum([cg_plane[turn, k, 8:9] for k in range(n_cmp)])
+        tail = pltpu.roll(jnp.broadcast_to(0.5 * tail, packed), 32, 1)
         swap_c.wait_recv()
-        across = normal_inverse(cg_total[...].reshape(packed))
+        folded = cg_total[...].reshape(16, LANES)
+        triangles = jnp.concatenate([folded, swap_halves(folded)], axis=0)
+        upper = jnp.where(lane > row, triangles, jnp.where(lane == row, 0.5 * triangles, 0.0))
+        upper = jnp.where(left, upper, 0.0)
+        lower = jnp.where(lane < row + 32, pltpu.roll(triangles, 32, 1), 0.0)
+        lower = jnp.where(lane == row + 32, tail, lower)
+        lower = jnp.where(lane < 32, 0.0, lower)
+        one_side = jnp.concatenate([upper, lower, jnp.zeros(full, jnp.float32)], axis=0)
+        compound_gram = (one_side + one_side.T)[:RANK]
+        gram_ref[...] = compound_gram
+        across = normal_inverse(compound_gram)
         others = cs_plane.at[turn, pl.ds(0, n_cmp - 1)]
         cs_all = remote(others, others, 7, cs_sems.at[turn], "cmp", me_c)
         cs_all.wait_recv()
@@ -360,10 +379,8 @@
         slot = lax.rem(me_t - peer + n_tgt, n_tgt) - 1
         remote(d_send, d_recv.at[slot], 9, recv_sems.at[9], "tgt", peer).start()
 
-    total = cg_total[...].reshape(packed)
-    other = swap_halves(total)
-    whole = jnp.concatenate([jnp.where(left, total, other), jnp.where(left, other, total)], axis=0)
-    diagonal = jnp.sum(jnp.where(pair, whole, 0.0), axis=0, keepdims=True)
+    alone = jnp.where(lane_of(full) == row_of(full), gram_ref[...], 0.0)
+    diagonal = jnp.sum(alone + swap_halves(alone), axis=0, keepdims=True)
     compound_count = 2 * half * n_cmp
     scaled = (raw_ref[...] / jnp.sqrt(diagonal / compound_count + 1e-06)).T
     compound_out[:, :half] = scaled[:RANK]
@@ -404,9 +421,10 @@
             vmem((16, LANES), f32),
             vmem((2, n_tgt // 2, 16, LANES), f32),
             vmem((2, 16, LANES), f32),
-            vmem((2, 16, LANES), f32),
+            vmem((2, 8, LANES), f32),
             vmem((2, n_cmp, 16, LANES), f32),
-            vmem((2, 16, LANES), f32),
+            vmem((2, 8, LANES), f32),
+            vmem((RANK, LANES), f32),
             vmem((PIECES, 8, LANES), f32),
             vmem((PIECES - 1, 8, LANES), f32),
             vmem((2, n_cmp, 8, LANES), f32),
@@ -423,7 +441,7 @@
             pltpu.SemaphoreType.DMA((2,)),
         ],
         compiler_params=pltpu.CompilerParams(
-            collective_id=0, has_side_effects=True, vmem_limit_bytes=62 * 1024 * 1024
+            collective_id=0, has_side_effects=True, vmem_limit_bytes=53 * 1024 * 1024
         ),
         cost_estimate=pl.CostEstimate(
             flops=2 * cmp_rows * tgt_rows * RANK * (cond_count + 2 * ITERS),

time: 139 us -> 128 us (0.921)
  Pallas kernels: 136 us -> 124 us
    pallas_call x1, Pallas kernels: 136 us -> 124 us  [body(): pl.pallas_call(functools.partial(kernel, n_cmp, n_tgt), out_shape=(jax.Sh...]
    unnamed x2 -> x6, local copies, waits for them, and re-layouts: 2.85 us -> 2.67 us
where the time goes in v3:
time: 128 us
  Pallas kernels  124 us (97%)
  local copies, waits for them, and re-layouts  2.67 us (2%)
    pallas_call x1, Pallas kernels, body(): pl.pallas_call(functools.partial(kernel, n_cmp, n_tgt), out_shape=(jax.Sh...  124 us
    unnamed x6, local copies, waits for them, and re-layouts  2.67 us

profile of v3, /device:TPU:1, one launch (start us, length us, event | category | flops | bytes accessed | tf_op | source)
XLA Modules:
  0.0 127.7 jit_solution(14642525141052332034)
XLA Ops:
  0.6 0.0 copy-start
  0.6 0.7 copy-done
  1.3 0.0 copy-start.1
  1.4 0.7 copy-done.1
  2.1 124.4 %shard_map.50 = (f32[64,256]{1,0:T(8,128)S(1)}, f32[64,64]{1,0:T(8,128)S(1)}) custom-call(bf16[256,64,128]{2,1,0:T(8,128)(2,1)} %x_hbm.1, bf16[64,64]{1,0:T(8,128)(2,1)S(1)} %copy-done, bf16[64,128]{1,0:T(8,128)(2,1)S(1)} %bitcast.3), custom_call_target="tpu_custom_call" | custom-call | flops 289406976 | bytes 4194304 | tf_op jit(solution)/shard_map/pallas_call | solution.py:404
  126.5 0.6 copy.7
  127.1 0.6 copy.8
Async XLA Ops:
  0.6 0.7 copy-start
  1.3 0.7 copy-start.1

commit v4 on v3

--- a/solution.py
+++ b/solution.py
@@ -11,6 +11,7 @@
 RANK = 64
 LANES = 128
 PIECES = 4
+TAIL = 6
 CHUNKS = 8
 HIGHEST = lax.Precision.HIGHEST
 
@@ -93,13 +94,10 @@
     n_cmp,
     n_tgt,
     x_hbm,
-    init_hbm,
-    cond_hbm,
+    small_ref,
     compound_out,
     target_out,
     x_ref,
-    init_ref,
-    cond_ref,
     inner,
     cond_gram,
     raw_ref,
@@ -150,12 +148,6 @@
             for h in range(2)
         ]
 
-    small = [
-        pltpu.make_async_copy(cond_hbm, cond_ref, x_sems.at[2 * CHUNKS]),
-        pltpu.make_async_copy(init_hbm, init_ref, x_sems.at[2 * CHUNKS + 1]),
-    ]
-    for one in small:
-        one.start()
     for c in range(CHUNKS):
         for one in fetch(c):
             one.start()
@@ -195,9 +187,7 @@
     pair = jnp.logical_or(lane_of(full) == row_of(full), lane_of(full) == row_of(full) + RANK)
     twice = pair.astype(jnp.bfloat16)
 
-    for one in small:
-        one.wait()
-    cond = cond_ref[...]
+    cond = small_ref[:, :LANES]
     cond_twice = lax.dot_general(
         cond, twice, (((0,), (0,)), ((), ())), preferred_element_type=jnp.float32
     )
@@ -211,7 +201,7 @@
     weights = jnp.concatenate(
         [jnp.where(wide_left, cond_twice, 0.0), jnp.where(wide_left, 0.0, cond_twice)], axis=0
     ).astype(jnp.bfloat16)
-    side_ref[...] = jnp.dot(init_ref[...], twice, preferred_element_type=jnp.float32)
+    side_ref[...] = jnp.dot(small_ref[:, LANES:], twice, preferred_element_type=jnp.float32)
 
     for c in range(CHUNKS):
         for one in fetch(c):
@@ -289,16 +279,17 @@
         raw_ref[...] = compound
 
         def add_rows(s, sums):
-            sums = list(sums)
             for d in range(8):
                 at = s * 8 + d
-                spread = jnp.broadcast_to(raw_ref[pl.ds(at, 1), :], (8, LANES))
-                for t in range(8):
-                    sums[t] = sums[t] + inner[at, 8 * t : 8 * t + 8, :] * spread
-            return tuple(sums)
-
-        zero = jnp.zeros((8, LANES), jnp.float32)
-        sums = lax.fori_loop(0, half // 8, add_rows, (zero,) * 8)
+                sums = sums + inner[at] * raw_ref[pl.ds(at, 1), :]
+            return sums
+
+        steps = half // 8
+        sums = lax.fori_loop(0, steps - TAIL, add_rows, jnp.zeros(full, jnp.float32))
+        for step in range(steps - TAIL, steps):
+            sums = add_rows(step, sums)
+        sums = [sums[8 * t : 8 * t + 8] for t in range(8)]
+        square = dot_f32(compound, compound, ((0,), (0,)))
         for p in range(PIECES):
             top = sums[p] + swap_halves(sums[p])
             bottom = sums[p + 4] + swap_halves(sums[p + 4])
@@ -308,7 +299,6 @@
             peer = me_c - me_x + x
             remote(cs_send.at[x], cs_recv.at[d - 1], 5, recv_sems.at[5], "cmp", peer).start()
 
-        square = dot_f32(compound, compound, ((0,), (0,)))
         upper = square[:32] + swap_halves(square[64:96])
         lower = pltpu.roll(square[32:64], 96, 1) + pltpu.roll(square[96:128], 32, 1)
         triangles = jnp.where(jnp.logical_and(lane < row, lane < 32), lower, upper)
@@ -373,7 +363,7 @@
         swap_c.wait_send()
 
     target = side_ref[...]
-    d_send[...] = tree_sum([target[8 * t : 8 * t + 8] * target[8 * t : 8 * t + 8] for t in range(8)])
+    d_send[...] = jnp.sum(target * target, axis=0, keepdims=True)
     for offset in line:
         peer = peer_at(me_t, offset, n_y, 2)
         slot = lax.rem(me_t - peer + n_tgt, n_tgt) - 1
@@ -387,8 +377,7 @@
     compound_out[:, half:] = scaled[RANK:]
 
     remote(d_recv, d_recv, 9, recv_sems.at[9], "tgt", mate).wait()
-    squares = tree_sum([d_send[...]] + [d_recv[k] for k in range(n_tgt - 1)])
-    diagonal = jnp.sum(squares, axis=0, keepdims=True)
+    diagonal = tree_sum([d_send[...]] + [d_recv[k] for k in range(n_tgt - 1)])
     target_count = RANK * n_tgt
     scaled = target / jnp.sqrt(diagonal / target_count + 1e-06)
     target_out[...] = scaled[:, :RANK]
@@ -407,12 +396,10 @@
             jax.ShapeDtypeStruct((RANK, cmp_rows), f32),
             jax.ShapeDtypeStruct((tgt_rows, RANK), f32),
         ),
-        in_specs=[pl.BlockSpec(memory_space=pltpu.HBM)] * 3,
+        in_specs=[pl.BlockSpec(memory_space=pltpu.HBM), pl.BlockSpec(memory_space=vmem)],
         out_specs=(pl.BlockSpec(memory_space=vmem), pl.BlockSpec(memory_space=vmem)),
         scratch_shapes=[
             vmem((cmp_rows, tgt_rows, cond_count), jnp.bfloat16),
-            vmem(target_init.shape, jnp.bfloat16),
-            vmem((RANK, cond_count), jnp.bfloat16),
             vmem((half, tgt_rows, LANES), f32),
             vmem((RANK, LANES), f32),
             vmem((half, LANES), f32),
@@ -431,9 +418,9 @@
             vmem((n_tgt, rows, LANES), f32),
             vmem((n_tgt - 1, rows, LANES), f32),
             vmem((n_tgt, rows, LANES), f32),
-            vmem((8, LANES), f32),
-            vmem((n_tgt - 1, 8, LANES), f32),
-            pltpu.SemaphoreType.DMA((2 * CHUNKS + 2,)),
+            vmem((1, LANES), f32),
+            vmem((n_tgt - 1, 1, LANES), f32),
+            pltpu.SemaphoreType.DMA((2 * CHUNKS,)),
             pltpu.SemaphoreType.DMA((10,)),
             pltpu.SemaphoreType.DMA((10,)),
             pltpu.SemaphoreType.DMA((2,)),
@@ -448,7 +435,7 @@
             bytes_accessed=2 * cmp_rows * tgt_rows * cond_count,
             transcendentals=0,
         ),
-    )(responses, target_init, condition_factor.T)
+    )(responses, jnp.concatenate([condition_factor.T, target_init], axis=1))
     return compound.T, target
 
 

time: 128 us -> 126 us (0.984)
  local copies, waits for them, and re-layouts: 2.67 us -> 1.25 us
    unnamed x6 -> x2, local copies, waits for them, and re-layouts: 2.67 us -> 1.25 us
where the time goes in v4:
time: 126 us
  Pallas kernels  123 us (98%)
    pallas_call x1, Pallas kernels, body(): pl.pallas_call(functools.partial(kernel, n_cmp, n_tgt), out_shape=(jax.Sh...  123 us

profile of v4, /device:TPU:1, one launch (start us, length us, event | category | flops | bytes accessed | tf_op | source)
XLA Modules:
  0.0 126.1 jit_solution(10855185916578273072)
XLA Ops:
  0.6 0.7 pad_maximum_fusion.small_ref
  1.4 123.5 %shard_map.50 = (f32[64,256]{1,0:T(8,128)S(1)}, f32[64,64]{1,0:T(8,128)S(1)}) custom-call(bf16[256,64,128]{2,1,0:T(8,128)(2,1)} %x_hbm.1, bf16[64,192]{1,0:T(8,128)(2,1)S(1)} %pad_maximum_fusion.small_ref), custom_call_target="tpu_custom_call" | custom-call | flops 289406976 | bytes 4194304 | tf_op jit(solution)/shard_map/pallas_call | solution.py:393
  124.9 0.6 copy.7
  125.5 0.6 copy.8

commit v5 on v4

--- a/solution.py
+++ b/solution.py
@@ -335,8 +335,9 @@
         lower = jnp.where(lane < row + 32, pltpu.roll(triangles, 32, 1), 0.0)
         lower = jnp.where(lane == row + 32, tail, lower)
         lower = jnp.where(lane < 32, 0.0, lower)
-        one_side = jnp.concatenate([upper, lower, jnp.zeros(full, jnp.float32)], axis=0)
-        compound_gram = (one_side + one_side.T)[:RANK]
+        one_side = jnp.concatenate([upper, lower], axis=0)
+        other = one_side.T[:RANK]
+        compound_gram = one_side + jnp.concatenate([other, jnp.zeros_like(other)], axis=1)
         gram_ref[...] = compound_gram
         across = normal_inverse(compound_gram)
         others = cs_plane.at[turn, pl.ds(0, n_cmp - 1)]

time: 126 us -> 126 us (level)
  no operation moved by 1% of the time
where the time goes in v5:
time: 126 us
  Pallas kernels  123 us (98%)
    pallas_call x1, Pallas kernels, body(): pl.pallas_call(functools.partial(kernel, n_cmp, n_tgt), out_shape=(jax.Sh...  123 us

profile of v5, /device:TPU:1, one launch (start us, length us, event | category | flops | bytes accessed | tf_op | source)
XLA Modules:
  0.0 126.0 jit_solution(7362192539568383310)
XLA Ops:
  0.6 0.7 pad_maximum_fusion.small_ref
  1.4 123.4 %shard_map.50 = (f32[64,256]{1,0:T(8,128)S(1)}, f32[64,64]{1,0:T(8,128)S(1)}) custom-call(bf16[256,64,128]{2,1,0:T(8,128)(2,1)} %x_hbm.1, bf16[64,192]{1,0:T(8,128)(2,1)S(1)} %pad_maximum_fusion.small_ref), custom_call_target="tpu_custom_call" | custom-call | flops 289406976 | bytes 4194304 | tf_op jit(solution)/shard_map/pallas_call | solution.py:394
  124.7 0.6 copy.7
  125.4 0.6 copy.8
